TPU v7x, 32 devices: a whole 2x2x4 slice. The times are simulated.
32 devices in a mesh: section: 4 (over y, core), ctx: 8 (over z, x).
Axes of the slice: x: 2, y: 2, z: 4, core: 2. Of those that a mesh axis runs over, the one named last changes fastest.
Arguments:
- section_input: bfloat16 [2, 1024, 2048], P(None, 'ctx'), may hold values from -6 to 6
- cotangent: bfloat16 [2, 1024, 2048], P(None, 'ctx'), may hold values from -6 to 6
- w_query: bfloat16 [4, 2048, 1024], P('section', 'ctx'), may hold values from -0.125 to 0.125
- w_key: bfloat16 [4, 2048, 1024], P('section', 'ctx'), may hold values from -0.125 to 0.125
- w_value: bfloat16 [4, 2048, 1024], P('section', 'ctx'), may hold values from -0.125 to 0.125
- w_out: bfloat16 [4, 1024, 2048], P('section', 'ctx'), may hold values from -0.1875 to 0.1875
- block_mask: int32 [2, 32, 2], P(None, 'ctx'), may hold values 0 or 1
Outputs:
- section_output: bfloat16 [4, 2, 1024, 2048], P('section', None, 'ctx')
- input_grad: bfloat16 [4, 2, 1024, 2048], P('section', None, 'ctx')
Inputs may be any that keep to these rules, and one draw needn't show every extreme that they name: A block always attends to itself; column 0 and 1 of block_mask choose its two neighbour blocks.
All inputs are finite; a program needn't handle non-finite values.
Results may differ from a plain program's by a relative error of at most 0.03.
Values may be sent and summed in bfloat16 or wider, within the bound.
A program may use at most 128 MiB of HBM per device.

v0:
```python
import jax
import jax.numpy as jnp
from jax import lax
from jax.sharding import PartitionSpec as P

D = 2048
HEADS = 8
HDIM = 128
BLOCKS_DEV = 4
BLK = 32


def padded(block, sides, width):
    for axis, dim in sides:
        count = lax.axis_size(axis)
        forward = [(i, i + 1) for i in range(count - 1)]
        backward = [(target, source) for source, target in forward]
        low = lax.ppermute(
            lax.slice_in_dim(block, block.shape[dim] - width, None, axis=dim), axis, forward
        )
        high = lax.ppermute(lax.slice_in_dim(block, 0, width, axis=dim), axis, backward)
        block = jnp.concatenate([low, block, high], axis=dim)
    return block


def shifted(block, axis, distance):
    devices = range(lax.axis_size(axis))
    route = [(i - distance, i) for i in devices if i - distance in devices]
    return lax.ppermute(block, axis, route)


def rms_scale(values):
    return values * lax.rsqrt(jnp.mean(values * values, axis=-1, keepdims=True) + 1e-06)


def allowed_keys(mask_rows, block_ids, block_count):
    mask_float = mask_rows.astype(jnp.float32)
    left = mask_float[:, 0] * (block_ids > 0).astype(jnp.float32)
    right = mask_float[:, 1] * (block_ids < block_count - 1).astype(jnp.float32)
    return jnp.stack([left, jnp.ones_like(left), right], axis=1)


def project(layer_in, w_query, w_key, w_value):
    length = layer_in.shape[0]
    normed = rms_scale(layer_in.astype(jnp.float32)).astype(jnp.bfloat16)

    def head_normed(weight):
        out = jnp.dot(normed, weight, preferred_element_type=jnp.float32)
        out = rms_scale(out.reshape(length, HEADS, HDIM))
        return out.reshape(length, HEADS * HDIM).astype(jnp.bfloat16)

    query = head_normed(w_query)
    key = head_normed(w_key)
    value = jnp.dot(normed, w_value, preferred_element_type=jnp.float32).astype(jnp.bfloat16)
    return (query, key, value)


def attend(query, keys_ext, values_ext, allow, layer_in, w_out):
    length = query.shape[0]
    nblock = length // BLK
    queries = query.reshape(nblock, BLK, HEADS, HDIM)

    def windows(extended):
        grid = extended.reshape(nblock + 2, BLK, HEADS, HDIM)
        return jnp.concatenate([grid[:-2], grid[1:-1], grid[2:]], axis=1)

    keys = windows(keys_ext)
    values = windows(values_ext)
    scores = jnp.einsum(
        "bqhd,bkhd->bhqk", queries, keys, preferred_element_type=jnp.float32
    ) * HDIM ** (-0.5)
    weight = jnp.repeat(allow, BLK, axis=1)[:, None, None, :]
    probs = jnp.exp(scores) * weight
    total = jnp.sum(probs, axis=-1)
    attended = jnp.einsum(
        "bhqk,bkhd->bqhd", probs.astype(jnp.bfloat16), values, preferred_element_type=jnp.float32
    )
    attended = attended / jnp.transpose(total, (0, 2, 1))[..., None]
    attended = attended.reshape(length, HEADS * HDIM).astype(jnp.bfloat16)
    update = jnp.dot(attended, w_out, preferred_element_type=jnp.float32)
    return (layer_in.astype(jnp.float32) + update).astype(jnp.bfloat16)


def put_slot(buffer, value, slot, active):
    return jnp.where(active, lax.dynamic_update_index_in_dim(buffer, value, slot, 0), buffer)


def take_slot(buffer, slot):
    return lax.dynamic_index_in_dim(buffer, slot, 0, keepdims=False)


def per_device(section_input, cotangent, w_query, w_key, w_value, w_out, block_mask):
    n_section = lax.axis_size("section")
    n_ctx = lax.axis_size("ctx")
    section = lax.axis_index("section")
    place = lax.axis_index("ctx")
    micro = section_input.shape[0]
    length = section_input.shape[1]
    width = HEADS * HDIM
    full_query, full_key, full_value, full_out = (
        lax.all_gather(w_query[0], "ctx", axis=0, tiled=True),
        lax.all_gather(w_key[0], "ctx", axis=0, tiled=True),
        lax.all_gather(w_value[0], "ctx", axis=0, tiled=True),
        lax.all_gather(w_out[0], "ctx", axis=0, tiled=True),
    )
    block_ids = place * BLOCKS_DEV + jnp.arange(BLOCKS_DEV)
    allows = jax.vmap(lambda rows_mask: allowed_keys(rows_mask, block_ids, BLOCKS_DEV * n_ctx))(
        block_mask
    )
    zero_rows = jnp.zeros((length, D), jnp.bfloat16)
    zero_heads = jnp.zeros((length, width), jnp.bfloat16)
    zero_wide = jnp.zeros((length + 2 * BLK, width), jnp.bfloat16)
    steps_total = n_section + micro - 1

    def run_project(values):
        return project(values, full_query, full_key, full_value)

    def skip_project(values):
        return (zero_heads, zero_heads, zero_heads)

    def run_attend(query, extended, layer_in, allow):
        return attend(query, extended[0], extended[1], allow, layer_in, full_out)

    def skip_attend(query, extended, layer_in, allow):
        return zero_rows

    kv_store = jnp.zeros((micro, 2, length, width), jnp.bfloat16)
    inputs = jnp.zeros((micro, length, D), jnp.bfloat16)
    outputs = jnp.zeros((micro, length, D), jnp.bfloat16)
    queries = jnp.zeros((micro, length, width), jnp.bfloat16)

    def forward_step(step, carry):
        incoming, inputs, outputs, queries, kv_store = carry
        micro_id = step - section
        active = (micro_id >= 0) & (micro_id < micro)
        slot = jnp.clip(micro_id, 0, micro - 1)
        layer_in = jnp.where(section == 0, take_slot(section_input, slot), incoming)
        query, key, value = lax.cond(active, run_project, skip_project, layer_in)
        local_kv = jnp.stack([key, value])
        extended = padded(local_kv, (("ctx", 1),), BLK)
        allow = take_slot(allows, slot)
        result = lax.cond(active, run_attend, skip_attend, query, extended, layer_in, allow)
        inputs = put_slot(inputs, layer_in, slot, active)
        outputs = put_slot(outputs, result, slot, active)
        queries = put_slot(queries, query, slot, active)
        kv_store = put_slot(kv_store, local_kv, slot, active)
        incoming = shifted(result, "section", 1)
        return (incoming, inputs, outputs, queries, kv_store)

    carry = (zero_rows, inputs, outputs, queries, kv_store)
    _, inputs, outputs, queries, kv_store = lax.fori_loop(0, steps_total, forward_step, carry)

    def pull_attend(query, extended, layer_in, allow, grad_in):

        def local_attend(query_in, keys_in, values_in, rows_in):
            return attend(query_in, keys_in, values_in, allow, rows_in, full_out)

        _, pull = jax.vjp(local_attend, query, extended[0], extended[1], layer_in)
        return pull(grad_in)

    def skip_pull(query, extended, layer_in, allow, grad_in):
        return (zero_heads, zero_wide, zero_wide, zero_rows)

    def pull_project(layer_in, d_query, own):
        _, pull = jax.vjp(run_project, layer_in)
        return pull((d_query, own[0], own[1]))[0]

    def skip_pull_project(layer_in, d_query, own):
        return zero_rows

    grads = jnp.zeros((micro, length, D), jnp.bfloat16)

    def backward_step(step, carry):
        incoming, grads = carry
        micro_id = step - (n_section - 1 - section)
        active = (micro_id >= 0) & (micro_id < micro)
        slot = jnp.clip(micro_id, 0, micro - 1)
        grad_in = jnp.where(section == n_section - 1, take_slot(cotangent, slot), incoming)
        layer_in = take_slot(inputs, slot)
        query = take_slot(queries, slot)
        extended = padded(take_slot(kv_store, slot), (("ctx", 1),), BLK)
        allow = take_slot(allows, slot)
        d_query, d_keys, d_values, d_direct = lax.cond(
            active, pull_attend, skip_pull, query, extended, layer_in, allow, grad_in
        )
        d_wide = jnp.stack([d_keys, d_values])
        rims = jnp.concatenate([d_wide[:, :BLK], d_wide[:, -BLK:]], axis=1)
        returned = padded(rims, (("ctx", 1),), BLK)
        own = d_wide[:, BLK:-BLK]
        own = own.at[:, :BLK].add(returned[:, :BLK])
        own = own.at[:, -BLK:].add(returned[:, -BLK:])
        d_projected = lax.cond(active, pull_project, skip_pull_project, layer_in, d_query, own)
        d_input = d_direct + d_projected
        grads = put_slot(grads, d_input, slot, active)
        incoming = shifted(d_input, "section", -1)
        return (incoming, grads)

    _, grads = lax.fori_loop(0, steps_total, backward_step, (zero_rows, grads))
    return (outputs[None], grads[None])


def solution(mesh):
    return jax.shard_map(
        per_device,
        mesh=mesh,
        in_specs=(
            P(None, "ctx", None),
            P(None, "ctx", None),
            P("section", "ctx", None),
            P("section", "ctx", None),
            P("section", "ctx", None),
            P("section", "ctx", None),
            P(None, "ctx", None),
        ),
        out_specs=(P("section", None, "ctx", None), P("section", None, "ctx", None)),
        check_vma=False,
    )
```

profile of v0, /device:TPU:16, one launch (start us, length us, event | category | flops | bytes accessed | tf_op | source)
XLA Modules:
  0.0 805.3 jit_solution(4391215996601857226)
XLA Ops:
  11.0 72.8 %all-gather.9.cloned.1.call-done = bf16[1,2048,1024]{2,1,0:T(8,128)(2,1)} async-done(((bf16[1,256,1024]{2,1,0:T(8,128)(2,1)}), bf16[1,2048,1024]{2,1,0:T(8,128)(2,1)}) %all-gather.9.cloned.1.call-update) | async-done | bytes 4194320 | tf_op jit(solution)/shard_map/all_gather | solution.py:101
  83.8 73.8 %all-gather.11.cloned.1.call-done = bf16[1,2048,1024]{2,1,0:T(8,128)(2,1)} async-done(((bf16[1,256,1024]{2,1,0:T(8,128)(2,1)}), bf16[1,2048,1024]{2,1,0:T(8,128)(2,1)}) %all-gather.11.cloned.1.call-update) | async-done | bytes 4194320 | tf_op jit(solution)/shard_map/all_gather | solution.py:102
  157.6 73.8 %all-gather.13.cloned.1.call-done = bf16[1,2048,1024]{2,1,0:T(8,128)(2,1)} async-done(((bf16[1,256,1024]{2,1,0:T(8,128)(2,1)}), bf16[1,2048,1024]{2,1,0:T(8,128)(2,1)}) %all-gather.13.cloned.1.call-update) | async-done | bytes 4194320 | tf_op jit(solution)/shard_map/all_gather | solution.py:103
  231.5 73.7 %all-gather.15.cloned.1.call-done = bf16[1,1024,2048]{2,1,0:T(8,128)(2,1)} async-done(((bf16[1,128,2048]{2,1,0:T(8,128)(2,1)}), bf16[1,1024,2048]{2,1,0:T(8,128)(2,1)}) %all-gather.15.cloned.1.call-update) | async-done | bytes 4194320 | tf_op jit(solution)/shard_map/all_gather | solution.py:104
  308.4 166.8 %while.41 = (s32[]{:T(128)}, bf16[128,2048]{1,0:T(8,128)(2,1)S(1)}, bf16[2,128,2048]{2,1,0:T(8,128)(2,1)S(1)}, bf16[2,128,2048]{2,1,0:T(8,128)(2,1)}, bf16[2,128...) while((s32[]{:T(128)}, bf16[128,2048]{1,0:T(8,128)(2,1)S(1)}, ...), condition=%wide.region_9.10_spmd, body=%wide.region_0.9_spmd.sunk | while | flops 2211841024 | bytes 75189416 | solution.py:151
  309.7 10.8 %conditional.8 = (bf16[128,1024]{1,0:T(8,128)(2,1)S(1)}, bf16[1,128,1024]{2,1,0:T(8,128)(2,1)S(1)}, bf16[1,128,1024]{2,1,0:T(8,128)(2,1)S(1)}) conditional(s32[]{:T(128)} %convert_element_type.301, () %tuple.200, (bf16[128,2048]{1,0:T(8,128)(2,1)S(1)}, bf16[2048,1024]{1,0:T(8,128)(2,1)}, bf16[2048,1024]{1,0:T(8,128)(2,1)}, ...), branch_computations={%region_1.1_spmd, %region_2.5_spmd} | conditional | flops 1614940288 | bytes 24972320 | solution.py:138
  331.1 6.6 conditional.9
  344.0 10.8 %conditional.8 = (bf16[128,1024]{1,0:T(8,128)(2,1)S(1)}, bf16[1,128,1024]{2,1,0:T(8,128)(2,1)S(1)}, bf16[1,128,1024]{2,1,0:T(8,128)(2,1)S(1)}) conditional(s32[]{:T(128)} %convert_element_type.301, () %tuple.200, (bf16[128,2048]{1,0:T(8,128)(2,1)S(1)}, bf16[2048,1024]{1,0:T(8,128)(2,1)}, bf16[2048,1024]{1,0:T(8,128)(2,1)}, ...), branch_computations={%region_1.1_spmd, %region_2.5_spmd} | conditional | flops 1614940288 | bytes 24972320 | solution.py:138
  365.2 6.6 conditional.9
  390.1 18.3 %collective-permute-start.2 = (bf16[128,2048]{1,0:T(8,128)(2,1)}, bf16[128,2048]{1,0:T(8,128)(2,1)S(1)}, u32[]{:S(2)}, u32[]{:S(2)}) collective-permute-start(bf16[128,2048]{1,0:T(8,128)(2,1)} %get-tuple-element.1251), channel_id=1, source_target_pairs={{0,8},{8,16},{16,24},{1,9},{9,17},{17,25},{2,10},{10,18},{18,26},{... | collective-permute-start | bytes 1572872 | tf_op jit(solution)/shard_map/while/body/eval_jaxpr/ppermute | solution.py:29
  424.4 7.3 collective-permute-start.2
  448.1 23.4 %collective-permute-start.2 = (bf16[128,2048]{1,0:T(8,128)(2,1)}, bf16[128,2048]{1,0:T(8,128)(2,1)S(1)}, u32[]{:S(2)}, u32[]{:S(2)}) collective-permute-start(bf16[128,2048]{1,0:T(8,128)(2,1)} %get-tuple-element.1251), channel_id=1, source_target_pairs={{0,8},{8,16},{16,24},{1,9},{9,17},{17,25},{2,10},{10,18},{18,26},{... | collective-permute-start | bytes 1572872 | tf_op jit(solution)/shard_map/while/body/eval_jaxpr/ppermute | solution.py:29
  477.2 321.6 %while.42 = (s32[]{:T(128)}, bf16[128,2048]{1,0:T(8,128)(2,1)}, bf16[2,128,2048]{2,1,0:T(8,128)(2,1)}, s32[]{:T(128)}, bf16[2,2,128,1024]{3,2,1,0:T(8,128)(2,1)}...) while((s32[]{:T(128)}, bf16[128,2048]{1,0:T(8,128)(2,1)}, ...), condition=%wide.region_24.25_spmd, body=%wide.region_10.24_spmd.sunk | while | flops 3389073152 | bytes 170649296 | solution.py:198
  503.5 7.3 collective-permute-done.7
  528.8 4.8 collective-permute-start.6
  540.9 11.4 %collective-permute-done.7 = bf16[128,2048]{1,0:T(8,128)(2,1)S(1)} collective-permute-done((bf16[128,2048]{1,0:T(8,128)(2,1)S(1)}, bf16[128,2048]{1,0:T(8,128)(2,1)S(1)}, u32[]{:S(2)}, u32[]{:S(2)}) %collective-permute-start.7) | collective-permute-done | bytes 524320 | tf_op jit(solution)/shard_map/while/body/eval_jaxpr/ppermute | solution.py:29
  570.2 4.8 collective-permute-start.6
  581.7 87.6 %collective-permute-done.7 = bf16[128,2048]{1,0:T(8,128)(2,1)S(1)} collective-permute-done((bf16[128,2048]{1,0:T(8,128)(2,1)S(1)}, bf16[128,2048]{1,0:T(8,128)(2,1)S(1)}, u32[]{:S(2)}, u32[]{:S(2)}) %collective-permute-start.7) | collective-permute-done | bytes 524320 | tf_op jit(solution)/shard_map/while/body/eval_jaxpr/ppermute | solution.py:29
  683.4 11.2 %conditional.10 = (bf16[128,1024]{1,0:T(8,128)(2,1)S(1)}, bf16[128,2048]{1,0:T(8,128)(2,1)S(1)}, bf16[1,192,1024]{2,1,0:T(8,128)(2,1)S(1)}, bf16[1,192,1024]{2,1,0:T(8,128)(2,1)S(1)}) conditional(s32[]{:T(128)} %convert_element_type.302, () %tuple.207, (pred[]{:T(512)}, bf16[2,128,2048]{2,1,0:T(8,128)(2,1)}, s32[]{:T(128)}, ...), branch_computations={%region_11.11_spmd, %region_12.14_spmd} | conditional | flops 691602432 | bytes 64605000 | solution.py:183
  706.3 18.6 %conditional.11 = (bf16[128,2048]{1,0:T(8,128)(2,1)S(1)}) conditional(s32[]{:T(128)} %convert_element_type.302, () %tuple.209, (bf16[2,192,1024]{2,1,0:T(8,128)(2,1)S(1)}, bf16[2,32,1024]{2,1,0:T(8,128)(2,1)S(1)}, bf16[2,32,1024]{2,1,0:T(8,128)(2,1)S(1)}, bf16[2048,1024]{1,0:T(8,128)(2,1)}, bf16[2,128,2048]{2,1,0:T(8,128)(2,1)S(1)}, ...), branch_computations={%region_15.15_spmd, %region_16.23_spmd} | conditional | flops 2693800704 | bytes 90314520 | solution.py:192
  728.4 7.9 collective-permute-done.7
  750.3 11.2 %conditional.10 = (bf16[128,1024]{1,0:T(8,128)(2,1)S(1)}, bf16[128,2048]{1,0:T(8,128)(2,1)S(1)}, bf16[1,192,1024]{2,1,0:T(8,128)(2,1)S(1)}, bf16[1,192,1024]{2,1,0:T(8,128)(2,1)S(1)}) conditional(s32[]{:T(128)} %convert_element_type.302, () %tuple.207, (pred[]{:T(512)}, bf16[2,128,2048]{2,1,0:T(8,128)(2,1)}, s32[]{:T(128)}, ...), branch_computations={%region_11.11_spmd, %region_12.14_spmd} | conditional | flops 691602432 | bytes 64605000 | solution.py:183
  765.3 4.8 collective-permute-start.6
  773.4 18.6 %conditional.11 = (bf16[128,2048]{1,0:T(8,128)(2,1)S(1)}) conditional(s32[]{:T(128)} %convert_element_type.302, () %tuple.209, (bf16[2,192,1024]{2,1,0:T(8,128)(2,1)S(1)}, bf16[2,32,1024]{2,1,0:T(8,128)(2,1)S(1)}, bf16[2,32,1024]{2,1,0:T(8,128)(2,1)S(1)}, bf16[2048,1024]{1,0:T(8,128)(2,1)}, bf16[2,128,2048]{2,1,0:T(8,128)(2,1)S(1)}, ...), branch_computations={%region_15.15_spmd, %region_16.23_spmd} | conditional | flops 2693800704 | bytes 90314520 | solution.py:192
  (524 shorter events, 320.7 us)
Async XLA Ops:
  7.2 76.6 %all-gather.9.cloned.1.call-start = ((), (), s32[]{:S(2)}) async-start(), calls=%async_computation | async-start | bytes 4718592 | tf_op jit(solution)/shard_map/all_gather | solution.py:101
  7.9 149.7 %all-gather.11.cloned.1.call-start = ((), (), s32[]{:S(2)}) async-start(), calls=%async_computation.1 | async-start | bytes 4718592 | tf_op jit(solution)/shard_map/all_gather | solution.py:102
  8.6 222.8 %all-gather.13.cloned.1.call-start = ((), (), s32[]{:S(2)}) async-start(), calls=%async_computation.2 | async-start | bytes 4718592 | tf_op jit(solution)/shard_map/all_gather | solution.py:103
  9.4 295.7 %all-gather.15.cloned.1.call-start = ((), (), s32[]{:S(2)}) async-start(), calls=%async_computation.3 | async-start | bytes 4718592 | tf_op jit(solution)/shard_map/all_gather | solution.py:104
  320.6 7.9 collective-permute-start
  354.9 8.3 %collective-permute-start = (bf16[2,32,1024]{2,1,0:T(8,128)(2,1)S(1)}, bf16[2,32,1024]{2,1,0:T(8,128)(2,1)S(1)}, u32[]{:S(2)}, u32[]{:S(2)}) collective-permute-start(bf16[2,32,1024]{2,1,0:T(8,128)(2,1)S(1)} %get-tuple-element.1248), channel_id=1, source_target_pairs={{1,0},{2,1},{3,2},{4,3},{5,4},{6,5},{7,6},{9,8},{10,9},{11,10},{12... | collective-permute-start | bytes 393224 | tf_op jit(solution)/shard_map/while/body/eval_jaxpr/ppermute | solution.py:21
  357.4 7.8 collective-permute-start.1
  378.3 7.9 collective-permute-start
  381.4 7.8 collective-permute-start.1
  390.1 22.0 %collective-permute-start.2 = (bf16[128,2048]{1,0:T(8,128)(2,1)}, bf16[128,2048]{1,0:T(8,128)(2,1)S(1)}, u32[]{:S(2)}, u32[]{:S(2)}) collective-permute-start(bf16[128,2048]{1,0:T(8,128)(2,1)} %get-tuple-element.1251), channel_id=1, source_target_pairs={{0,8},{8,16},{16,24},{1,9},{9,17},{17,25},{2,10},{10,18},{18,26},{... | collective-permute-start | bytes 1572872 | tf_op jit(solution)/shard_map/while/body/eval_jaxpr/ppermute | solution.py:29
  413.7 7.9 collective-permute-start
  415.6 7.8 collective-permute-start.1
  424.4 11.0 %collective-permute-start.2 = (bf16[128,2048]{1,0:T(8,128)(2,1)}, bf16[128,2048]{1,0:T(8,128)(2,1)S(1)}, u32[]{:S(2)}, u32[]{:S(2)}) collective-permute-start(bf16[128,2048]{1,0:T(8,128)(2,1)} %get-tuple-element.1251), channel_id=1, source_target_pairs={{0,8},{8,16},{16,24},{1,9},{9,17},{17,25},{2,10},{10,18},{18,26},{... | collective-permute-start | bytes 1572872 | tf_op jit(solution)/shard_map/while/body/eval_jaxpr/ppermute | solution.py:29
  436.9 7.9 collective-permute-start
  448.1 27.1 %collective-permute-start.2 = (bf16[128,2048]{1,0:T(8,128)(2,1)}, bf16[128,2048]{1,0:T(8,128)(2,1)S(1)}, u32[]{:S(2)}, u32[]{:S(2)}) collective-permute-start(bf16[128,2048]{1,0:T(8,128)(2,1)} %get-tuple-element.1251), channel_id=1, source_target_pairs={{0,8},{8,16},{16,24},{1,9},{9,17},{17,25},{2,10},{10,18},{18,26},{... | collective-permute-start | bytes 1572872 | tf_op jit(solution)/shard_map/while/body/eval_jaxpr/ppermute | solution.py:29
  480.2 7.8 collective-permute-start.4
  502.2 8.6 %collective-permute-start.7 = (bf16[128,2048]{1,0:T(8,128)(2,1)S(1)}, bf16[128,2048]{1,0:T(8,128)(2,1)S(1)}, u32[]{:S(2)}, u32[]{:S(2)}) collective-permute-start(bf16[128,2048]{1,0:T(8,128)(2,1)S(1)} %get-tuple-element.1276), channel_id=1, source_target_pairs={{8,0},{16,8},{24,16},{9,1},{17,9},{25,17},{10,2},{18,10},{26,18},{... | collective-permute-start | bytes 1572872 | tf_op jit(solution)/shard_map/while/body/eval_jaxpr/ppermute | solution.py:29
  528.8 8.6 %collective-permute-start.6 = (bf16[2,32,1024]{2,1,0:T(8,128)(2,1)S(1)}, bf16[2,32,1024]{2,1,0:T(8,128)(2,1)S(1)}, u32[]{:S(2)}, u32[]{:S(2)}) collective-permute-start(bf16[2,32,1024]{2,1,0:T(8,128)(2,1)S(1)} %get-tuple-element.1274), channel_id=1, source_target_pairs={{1,0},{2,1},{3,2},{4,3},{5,4},{6,5},{7,6},{9,8},{10,9},{11,10},{12... | collective-permute-start | bytes 393224 | tf_op jit(solution)/shard_map/while/body/eval_jaxpr/ppermute | solution.py:21
  539.6 12.6 %collective-permute-start.7 = (bf16[128,2048]{1,0:T(8,128)(2,1)S(1)}, bf16[128,2048]{1,0:T(8,128)(2,1)S(1)}, u32[]{:S(2)}, u32[]{:S(2)}) collective-permute-start(bf16[128,2048]{1,0:T(8,128)(2,1)S(1)} %get-tuple-element.1276), channel_id=1, source_target_pairs={{8,0},{16,8},{24,16},{9,1},{17,9},{25,17},{10,2},{18,10},{26,18},{... | collective-permute-start | bytes 1572872 | tf_op jit(solution)/shard_map/while/body/eval_jaxpr/ppermute | solution.py:29
  570.2 8.0 collective-permute-start.6
  580.4 88.9 %collective-permute-start.7 = (bf16[128,2048]{1,0:T(8,128)(2,1)S(1)}, bf16[128,2048]{1,0:T(8,128)(2,1)S(1)}, u32[]{:S(2)}, u32[]{:S(2)}) collective-permute-start(bf16[128,2048]{1,0:T(8,128)(2,1)S(1)} %get-tuple-element.1276), channel_id=1, source_target_pairs={{8,0},{16,8},{24,16},{9,1},{17,9},{25,17},{10,2},{18,10},{26,18},{... | collective-permute-start | bytes 1572872 | tf_op jit(solution)/shard_map/while/body/eval_jaxpr/ppermute | solution.py:29
  698.4 8.0 collective-permute-start.6
  727.1 9.2 %collective-permute-start.7 = (bf16[128,2048]{1,0:T(8,128)(2,1)S(1)}, bf16[128,2048]{1,0:T(8,128)(2,1)S(1)}, u32[]{:S(2)}, u32[]{:S(2)}) collective-permute-start(bf16[128,2048]{1,0:T(8,128)(2,1)S(1)} %get-tuple-element.1276), channel_id=1, source_target_pairs={{8,0},{16,8},{24,16},{9,1},{17,9},{25,17},{10,2},{18,10},{26,18},{... | collective-permute-start | bytes 1572872 | tf_op jit(solution)/shard_map/while/body/eval_jaxpr/ppermute | solution.py:29
  765.3 8.0 collective-permute-start.6
  (62 other events, 221.6 us)
Sparse Core Ops, SparseCore 0:
  10.1 73.6 all-gather.8
  85.9 71.6 all-gather.10
  159.8 71.6 all-gather.12
  233.4 71.6 all-gather.14
where the time goes:
time: 810 us; the launch traced here: 805 us
  waiting for transfers between devices  468 us (58%)
  starting transfers between devices  153 us (19%)
  matrix products  59.4 us (7%)
  local copies, waits for them, and re-layouts  56.4 us (7%)
  other arithmetic  52.1 us (6%)
  between operations  13.8 us (2%)
    ppermute x10, waiting for transfers between devices, shifted(): return lax.ppermute(block, axis, route)  117 us
    all_gather x1, waiting for transfers between devices, per_device(): lax.all_gather(w_value[0], 'ctx', axis=0, tiled=True)  73.8 us
    all_gather x1, waiting for transfers between devices, per_device(): lax.all_gather(w_key[0], 'ctx', axis=0, tiled=True)  73.8 us
    all_gather x1, waiting for transfers between devices, per_device(): lax.all_gather(w_out[0], 'ctx', axis=0, tiled=True)  73.7 us
    all_gather x1, waiting for transfers between devices, per_device(): lax.all_gather(w_query[0], 'ctx', axis=0, tiled=True)  72.8 us
    ppermute x10, starting transfers between devices, shifted(): return lax.ppermute(block, axis, route)  58 us
    ppermute x15, starting transfers between devices, padded(): lax.ppermute(lax.slice_in_dim(block, 0, width, axis=dim), axis, backward)  54.8 us
    select_n x25, other arithmetic, put_slot(): jnp.where(active, lax.dynamic_update_index_in_dim(buffer, value, slot, 0)...  46.2 us
  transfers between devices with their start and end apart: 44, of which 35 were waited for; matrix products, arithmetic and copies ran while one was open for 4% of the time, Pallas kernels for 0%

commit v1 on v0

v1 whole, which is shorter than its diff:
```python
import functools

import jax
import jax.numpy as jnp
from jax import lax
from jax.experimental import pallas as pl
from jax.experimental.pallas import tpu as pltpu
from jax.sharding import PartitionSpec as P

D = 2048
HEADS = 8
HDIM = 128
WIDTH = HEADS * HDIM
BLK = 32
EPS = 1e-06
EXT = 256
STEP = 512
MESH = pl.DeviceIdType.MESH
F32 = jnp.float32
BF16 = jnp.bfloat16


def grid_of(n_ctx):
    wide = 1
    while (2 * wide) * (2 * wide) * 2 <= n_ctx:
        wide *= 2
    return n_ctx // wide, wide


def dot(a, b, dims=((1,), (0,))):
    return lax.dot_general(a, b, (dims, ((), ())), preferred_element_type=F32)


def head_mean(values):
    return jnp.mean(values, axis=-1, keepdims=True)


def kernel(
    n_section, n_ctx, micro, length,
    x0_ref, cot_ref, wq_in, wk_in, wv_in, wo_in, mask_ref,
    out_ref, grad_ref,
    wq, wk, wv, wo, xbuf, gbuf, nbuf, qbuf, rq, rk, kv, att, inv_total, probs,
    datt, dq, dkv, rims, dn,
    g_recv, g_send, own_sem, x_recv, x_send, b_recv, b_send, h_recv, h_send, r_recv, r_send, in_sem,
):
    section = lax.axis_index("section")
    place = lax.axis_index("ctx")
    tall, wide = grid_of(n_ctx)
    z = place // wide
    x = place % wide
    rows_all = micro * length

    around = (
        (z + 1 < tall, {"ctx": place + wide}),
        (z > 0, {"ctx": place - wide}),
        (x + 1 < wide, {"ctx": place + 1}),
        (x > 0, {"ctx": place - 1}),
    )
    has_right, right = place + 1 < n_ctx, {"ctx": place + 1}
    has_left, left = place > 0, {"ctx": place - 1}
    has_next, following = section + 1 < n_section, {"section": section + 1}
    has_prev, previous = section > 0, {"section": section - 1}

    barrier = pltpu.get_barrier_semaphore()
    friends = around + ((has_right, right), (has_left, left), (has_next, following), (has_prev, previous))
    count = 0
    for there, device in friends:
        @pl.when(there)
        def _(device=device):
            pl.semaphore_signal(barrier, inc=1, device_id=device, device_id_type=MESH)
        count = count + there.astype(jnp.int32)
    pl.semaphore_wait(barrier, count)

    weights = ((wk_in, wk, False), (wv_in, wv, False), (wq_in, wq, False), (wo_in, wo, True))

    def part(a, shard):
        rows = weights[a][0].shape[0]
        return weights[a][1].at[pl.ds(pl.multiple_of(shard * rows, rows), rows), :]

    def hop(a, shard, way, own):
        there, device = around[way]
        return there, pltpu.make_async_remote_copy(
            src_ref=weights[a][0] if own else part(a, shard),
            dst_ref=part(a, shard),
            send_sem=g_send.at[a, shard, way],
            recv_sem=g_recv.at[a, shard],
            device_id=device,
            device_id_type=MESH,
        )

    def ways_on(x_first, dz, dx):
        along_z = (0,) if dz > 0 else (1,)
        along_x = (2,) if dx > 0 else (3,)
        if x_first:
            return along_z if dz else along_x + (0, 1)
        return along_x if dx else along_z + (2, 3)

    offsets = [
        (dz, dx)
        for dz in range(1 - tall, tall)
        for dx in range(1 - wide, wide)
        if (dz, dx) != (0, 0)
    ]
    offsets.sort(key=lambda o: (abs(o[0]) + abs(o[1]), o))

    def gather(first):
        for a in range(4):
            for way in range(4):
                there, copy = hop(a, place, way, True)

                @pl.when(there)
                def _(copy=copy):
                    copy.start() if first else copy.wait_send()
        for dz, dx in offsets:
            zs, xs = z - dz, x - dx
            inside = (zs >= 0) & (zs < tall) & (xs >= 0) & (xs < wide)

            @pl.when(inside)
            def _(dz=dz, dx=dx, shard=zs * wide + xs):
                for a in range(4):
                    if first:
                        hop(a, shard, 0, False)[1].wait_recv()
                    for way in ways_on(weights[a][2], dz, dx):
                        there, copy = hop(a, shard, way, False)

                        @pl.when(there)
                        def _(copy=copy):
                            copy.start() if first else copy.wait_send()

    own_copies = [
        pltpu.make_async_copy(weights[a][0], part(a, place), own_sem.at[a]) for a in range(4)
    ]
    x_copy = pltpu.make_async_copy(x0_ref, xbuf, in_sem.at[0])
    g_copy = pltpu.make_async_copy(cot_ref, gbuf, in_sem.at[1])
    for copy in own_copies:
        copy.start()

    @pl.when(section == 0)
    def _():
        x_copy.start()

    @pl.when(section == n_section - 1)
    def _():
        g_copy.start()

    kv[...] = jnp.zeros_like(kv)
    rims[...] = jnp.zeros_like(rims)
    gather(True)
    for copy in own_copies:
        copy.wait()

    def relay(source, target, send, recv, device, c):
        cols = pl.ds(c * STEP, STEP)
        return pltpu.make_async_remote_copy(
            src_ref=source.at[:, cols], dst_ref=target.at[:, cols],
            send_sem=send.at[c], recv_sem=recv.at[c], device_id=device, device_id_type=MESH,
        )

    n_relay = D // STEP

    @pl.when(section == 0)
    def _():
        x_copy.wait()

    @pl.when(has_prev)
    def _():
        for c in range(n_relay):
            relay(out_ref, xbuf, x_send, x_recv, previous, c).wait_recv()

    chunk = 64

    @pl.loop(0, rows_all // chunk)
    def _(i):
        rows = pl.ds(pl.multiple_of(i * chunk, chunk), chunk)
        values = xbuf[rows, :].astype(F32)
        nbuf[rows, :] = (values * lax.rsqrt(head_mean(values * values) + EPS)).astype(BF16)

    def norm_heads(values):
        scales = []
        for h in range(STEP // HDIM):
            one = values[:, h * HDIM:(h + 1) * HDIM]
            scale = lax.rsqrt(head_mean(one * one) + EPS)
            scales.append(jnp.broadcast_to(scale, one.shape))
        return jnp.concatenate(scales, axis=1)

    @pl.loop(0, WIDTH // STEP)
    def _(i):
        cols = pl.ds(pl.multiple_of(i * STEP, STEP), STEP)
        out = dot(nbuf[...], wk[:, cols])
        scale = norm_heads(out)
        rk[:, cols] = scale
        key = (out * scale).astype(BF16)
        for m in range(micro):
            kv[0, m, BLK:BLK + length, cols] = key[m * length:(m + 1) * length]
        value = dot(nbuf[...], wv[:, cols]).astype(BF16)
        for m in range(micro):
            kv[1, m, BLK:BLK + length, cols] = value[m * length:(m + 1) * length]

    def to_right():
        return pltpu.make_async_remote_copy(
            src_ref=kv.at[:, :, pl.ds(length, BLK), :], dst_ref=kv.at[:, :, pl.ds(0, BLK), :],
            send_sem=h_send.at[0], recv_sem=h_recv.at[0], device_id=right, device_id_type=MESH,
        )

    def to_left():
        return pltpu.make_async_remote_copy(
            src_ref=kv.at[:, :, pl.ds(BLK, BLK), :], dst_ref=kv.at[:, :, pl.ds(BLK + length, BLK), :],
            send_sem=h_send.at[1], recv_sem=h_recv.at[1], device_id=left, device_id_type=MESH,
        )

    @pl.when(has_right)
    def _():
        to_right().start()

    @pl.when(has_left)
    def _():
        to_left().start()

    @pl.loop(0, WIDTH // STEP)
    def _(i):
        cols = pl.ds(pl.multiple_of(i * STEP, STEP), STEP)
        out = dot(nbuf[...], wq[:, cols])
        scale = norm_heads(out)
        rq[:, cols] = scale
        qbuf[:, cols] = (out * scale).astype(BF16)

    @pl.when(has_left)
    def _():
        to_right().wait_recv()

    @pl.when(has_right)
    def _():
        to_left().wait_recv()

    @pl.loop(0, HEADS)
    def _(h):
        cols = pl.ds(pl.multiple_of(h * HDIM, HDIM), HDIM)
        for m in range(micro):
            rows = slice(m * length, (m + 1) * length)
            scores = dot(qbuf[rows, cols], kv[0, m, :, cols], ((1,), (1,))) * HDIM ** (-0.5)
            prob = jnp.exp(scores) * mask_ref[m]
            probs[m, h] = prob
            inv = 1.0 / jnp.sum(prob, axis=-1, keepdims=True)
            inv_total[rows, cols] = jnp.broadcast_to(inv, (length, HDIM))
            att[rows, cols] = (dot(prob.astype(BF16), kv[1, m, :, cols]) * inv).astype(BF16)

    for c in range(n_relay):
        cols = slice(c * STEP, (c + 1) * STEP)
        update = dot(att[...], wo[:, cols])
        out_ref[:, cols] = (xbuf[:, cols].astype(F32) + update).astype(BF16)

        @pl.when(has_next)
        def _(c=c):
            relay(out_ref, xbuf, x_send, x_recv, following, c).start()

    @pl.when(section == n_section - 1)
    def _():
        g_copy.wait()

    @pl.when(has_next)
    def _():
        for c in range(n_relay):
            relay(grad_ref, gbuf, b_send, b_recv, following, c).wait_recv()

    @pl.loop(0, WIDTH // STEP)
    def _(i):
        cols = pl.ds(pl.multiple_of(i * STEP, STEP), STEP)
        datt[:, cols] = dot(gbuf[...], wo[cols, :], ((1,), (1,))).astype(BF16)

    @pl.loop(0, HEADS)
    def _(h):
        cols = pl.ds(pl.multiple_of(h * HDIM, HDIM), HDIM)
        for m in range(micro):
            rows = slice(m * length, (m + 1) * length)
            prob = probs[m, h]
            d_att = datt[rows, cols].astype(F32)
            inv = inv_total[rows, cols]
            d_sum = (d_att * inv)
            d_total = jnp.sum(d_sum * att[rows, cols].astype(F32), axis=-1, keepdims=True)
            d_sum = d_sum.astype(BF16)
            d_prob = dot(d_sum, kv[1, m, :, cols], ((1,), (1,))) - d_total
            d_score = (d_prob * prob * HDIM ** (-0.5)).astype(BF16)
            dkv[1, m, :, cols] = dot(prob.astype(BF16), d_sum, ((0,), (0,))).astype(BF16)
            dkv[0, m, :, cols] = dot(d_score, qbuf[rows, cols], ((0,), (0,))).astype(BF16)
            d_query = dot(d_score, kv[0, m, :, cols])
            query = qbuf[rows, cols].astype(F32)
            d_query = (d_query - query * head_mean(d_query * query)) * rq[rows, cols]
            dq[rows, cols] = d_query.astype(BF16)

    def rim_left():
        return pltpu.make_async_remote_copy(
            src_ref=dkv.at[:, :, pl.ds(0, BLK), :], dst_ref=rims.at[1],
            send_sem=r_send.at[0], recv_sem=r_recv.at[0], device_id=left, device_id_type=MESH,
        )

    def rim_right():
        return pltpu.make_async_remote_copy(
            src_ref=dkv.at[:, :, pl.ds(BLK + length, BLK), :], dst_ref=rims.at[0],
            send_sem=r_send.at[1], recv_sem=r_recv.at[1], device_id=right, device_id_type=MESH,
        )

    @pl.when(has_left)
    def _():
        rim_left().start()

    @pl.when(has_right)
    def _():
        rim_right().start()

    @pl.loop(0, D // STEP)
    def _(i):
        cols = pl.ds(pl.multiple_of(i * STEP, STEP), STEP)
        dn[:, cols] = dot(dq[...], wq[cols, :], ((1,), (1,)))

    @pl.when(has_right)
    def _():
        rim_left().wait_recv()

    @pl.when(has_left)
    def _():
        rim_right().wait_recv()

    for which in range(2):
        for m in range(micro):
            for side, start in ((0, BLK), (1, length)):
                rows = slice(start, start + BLK)
                dkv[which, m, rows] = dkv[which, m, rows] + rims[side, which, m]

    @pl.loop(0, HEADS)
    def _(h):
        cols = pl.ds(pl.multiple_of(h * HDIM, HDIM), HDIM)
        for m in range(micro):
            rows = slice(m * length, (m + 1) * length)
            d_key = dkv[0, m, BLK:BLK + length, cols].astype(F32)
            key = kv[0, m, BLK:BLK + length, cols].astype(F32)
            d_key = (d_key - key * head_mean(d_key * key)) * rk[rows, cols]
            dq[rows, cols] = d_key.astype(BF16)
            datt[rows, cols] = dkv[1, m, BLK:BLK + length, cols]

    @pl.loop(0, D // STEP)
    def _(i):
        cols = pl.ds(pl.multiple_of(i * STEP, STEP), STEP)
        dn[:, cols] = (
            dn[:, cols]
            + dot(dq[...], wk[cols, :], ((1,), (1,)))
            + dot(datt[...], wv[cols, :], ((1,), (1,)))
        )

    @pl.loop(0, rows_all // chunk)
    def _(i):
        rows = pl.ds(pl.multiple_of(i * chunk, chunk), chunk)
        values = xbuf[rows, :].astype(F32)
        scale = lax.rsqrt(head_mean(values * values) + EPS)
        d_norm = dn[rows, :].astype(BF16).astype(F32)
        normed = values * scale
        d_in = scale * (d_norm - normed * head_mean(d_norm * normed))
        grad_ref[rows, :] = (gbuf[rows, :].astype(F32) + d_in.astype(BF16).astype(F32)).astype(BF16)

    @pl.when(has_prev)
    def _():
        for c in range(n_relay):
            relay(grad_ref, gbuf, b_send, b_recv, previous, c).start()

    gather(False)

    @pl.when(has_next)
    def _():
        for c in range(n_relay):
            relay(out_ref, xbuf, x_send, x_recv, following, c).wait_send()

    @pl.when(has_right)
    def _():
        to_right().wait_send()
        rim_right().wait_send()

    @pl.when(has_left)
    def _():
        to_left().wait_send()
        rim_left().wait_send()

    @pl.when(has_prev)
    def _():
        for c in range(n_relay):
            relay(grad_ref, gbuf, b_send, b_recv, previous, c).wait_send()


def mask_weights(block_mask, place, n_ctx, length):
    blocks = length // BLK
    ids = place * blocks + jnp.arange(blocks)
    mask = block_mask.astype(F32)
    before = mask[:, :, 0] * (ids > 0).astype(F32)
    after = mask[:, :, 1] * (ids < blocks * n_ctx - 1).astype(F32)
    offset = jnp.arange(EXT)[None, :] // BLK - jnp.arange(length)[:, None] // BLK
    def rows(values):
        return jnp.repeat(values, BLK, axis=1)[:, :, None]
    return jnp.where(offset == 0, rows(before), jnp.where(offset == 1, 1.0, jnp.where(offset == 2, rows(after), 0.0)))


def per_device(n_section, n_ctx, section_input, cotangent, w_query, w_key, w_value, w_out, block_mask):
    micro, length = section_input.shape[:2]
    rows = micro * length
    mask = mask_weights(block_mask, lax.axis_index("ctx"), n_ctx, length)
    any_space = pl.BlockSpec(memory_space=pl.ANY)
    vmem = pl.BlockSpec(memory_space=pltpu.VMEM)
    dma = pltpu.SemaphoreType.DMA
    n_relay = D // STEP
    out, grad = pl.pallas_call(
        functools.partial(kernel, n_section, n_ctx, micro, length),
        out_shape=[jax.ShapeDtypeStruct((rows, D), BF16)] * 2,
        in_specs=[any_space] * 6 + [vmem],
        out_specs=[vmem, vmem],
        scratch_shapes=[
            pltpu.VMEM((D, WIDTH), BF16),
            pltpu.VMEM((D, WIDTH), BF16),
            pltpu.VMEM((D, WIDTH), BF16),
            pltpu.VMEM((WIDTH, D), BF16),
            pltpu.VMEM((rows, D), BF16),
            pltpu.VMEM((rows, D), BF16),
            pltpu.VMEM((rows, D), BF16),
            pltpu.VMEM((rows, WIDTH), BF16),
            pltpu.VMEM((rows, WIDTH), F32),
            pltpu.VMEM((rows, WIDTH), F32),
            pltpu.VMEM((2, micro, EXT, WIDTH), BF16),
            pltpu.VMEM((rows, WIDTH), BF16),
            pltpu.VMEM((rows, WIDTH), F32),
            pltpu.VMEM((micro, HEADS, length, EXT), F32),
            pltpu.VMEM((rows, WIDTH), BF16),
            pltpu.VMEM((rows, WIDTH), BF16),
            pltpu.VMEM((2, micro, EXT, WIDTH), BF16),
            pltpu.VMEM((2, 2, micro, BLK, WIDTH), BF16),
            pltpu.VMEM((rows, D), F32),
            dma((4, n_ctx)),
            dma((4, n_ctx, 4)),
            dma((4,)),
            dma((n_relay,)),
            dma((n_relay,)),
            dma((n_relay,)),
            dma((n_relay,)),
            dma((2,)),
            dma((2,)),
            dma((2,)),
            dma((2,)),
            dma((2,)),
        ],
        compiler_params=pltpu.CompilerParams(
            collective_id=0, has_side_effects=True, vmem_limit_bytes=56 * 2**20
        ),
    )(
        section_input.reshape(rows, D), cotangent.reshape(rows, D),
        w_query[0], w_key[0], w_value[0], w_out[0], mask,
    )
    return out.reshape(1, micro, length, D), grad.reshape(1, micro, length, D)


def solution(mesh):
    return jax.shard_map(
        functools.partial(per_device, mesh.shape["section"], mesh.shape["ctx"]),
        mesh=mesh,
        in_specs=(
            P(None, "ctx", None),
            P(None, "ctx", None),
            P("section", "ctx", None),
            P("section", "ctx", None),
            P("section", "ctx", None),
            P("section", "ctx", None),
            P(None, "ctx", None),
        ),
        out_specs=(P("section", None, "ctx", None), P("section", None, "ctx", None)),
        check_vma=False,
    )
```

time: 810 us -> 366 us (0.45)
  waiting for transfers between devices: 468 us -> 0 us
  Pallas kernels: 0 us -> 360 us
  starting transfers between devices: 153 us -> 0 us
  matrix products: 59.4 us -> 0 us
  local copies, waits for them, and re-layouts: 56.4 us -> 4.35 us
  other arithmetic: 52.1 us -> 0.99 us
  between operations: 13.8 us -> 0.7 us
    pallas_call x0 -> x1, Pallas kernels: none -> 360 us  [per_device(): pl.pallas_call(functools.partial(kernel, n_section, n_ctx, micro, length)...]
    all_gather x4 -> x0, waiting for transfers between devices: 294 us -> none  [the longest x1 73.8 us: per_device(): lax.all_gather(w_value[0], 'ctx', axis=0, tiled=True)]
    ppermute x40 -> x0, waiting for transfers between devices: 171 us -> none  [the longest x10 117 us: shifted(): return lax.ppermute(block, axis, route)]
    ppermute x40 -> x0, starting transfers between devices: 153 us -> none  [the longest x10 58 us: shifted(): return lax.ppermute(block, axis, route)]
    dot_general x36 -> x0, matrix products: 59.4 us -> none  [the longest x12 36.3 us: head_normed(): out = jnp.dot(normed, weight, preferred_element_type=jnp.float32)]
    select_n x27 -> x3, other arithmetic: 46.3 us -> 0.85 us  [the longest x1 0.84 us: mask_weights(): jnp.where(offset == 0, rows(before), jnp.where(offset == 1, 1.0, jnp.wher...]
    cond x122 -> x0, local copies, waits for them, and re-layouts: 15.4 us -> none
    another operation x30 -> x0, local copies, waits for them, and re-layouts: 10.6 us -> none  [the longest x15 8.01 us: backward_step(): d_wide = jnp.stack([d_keys, d_values])]
  transfers between devices with their start and end apart: 44 -> 0, of which waited for: 35 -> 0; matrix products, arithmetic and copies ran while one was open for 4% -> 0% of each run, Pallas kernels for 0% -> 0%
where the time goes in v1:
time: 366 us
  Pallas kernels  360 us (98%)
  local copies, waits for them, and re-layouts  4.35 us (1%)
    pallas_call x1, Pallas kernels, per_device(): pl.pallas_call(functools.partial(kernel, n_section, n_ctx, micro, length)...  360 us

profile of v1, /device:TPU:16, one launch (start us, length us, event | category | flops | bytes accessed | tf_op | source)
XLA Modules:
  0.0 365.7 jit_solution(1384242114772570682)
XLA Ops:
  0.7 0.0 copy-start.1
  0.7 0.7 copy-done.1
  1.4 0.1 broadcast_in_dim.57
  1.4 0.1 broadcast_in_dim.58
  1.5 0.1 broadcast_in_dim.51
  1.6 0.1 broadcast_in_dim.52
  1.7 0.1 subtract_compare_fusion.2
  1.8 0.8 select_select_fusion.mask_ref
  2.7 359.7 %shard_map.86 = (bf16[256,2048]{1,0:T(8,128)(2,1)}, bf16[256,2048]{1,0:T(8,128)(2,1)}) custom-call(bf16[256,2048]{1,0:T(8,128)(2,1)} %bitcast.10, bf16[256,2048]{1,0:T(8,128)(2,1)} %bitcast.11, bf16[256,1024]{1,0:T(8,128)(2,1)} %bitcast.14, bf16[256,1024]{1,0:T(8,128)(2,1)} %bitcast.15, bf16[256,1024]{1,0:T(8,128)(2,1)} %bitcast.16, ...), custom_call_target="tpu_custom_call" | custom-call | tf_op jit(solution)/shard_map/pallas_call | solution.py:407
  362.3 0.0 copy-start
  362.3 2.4 copy.11
  364.7 0.0 copy-done
  364.7 1.0 copy.12
  (7 shorter events, 0.0 us)
Async XLA Ops:
  0.7 0.7 copy-start.1
  362.3 2.4 copy-start

commit v2 on v1

--- a/solution.py
+++ b/solution.py
@@ -71,16 +71,25 @@
         count = count + there.astype(jnp.int32)
     pl.semaphore_wait(barrier, count)
 
-    weights = ((wk_in, wk, False), (wv_in, wv, False), (wq_in, wq, False), (wo_in, wo, True))
+    deep, half = wk_in.shape[0], wo_in.shape[0] // 2
+    weights = (
+        (wk_in, wk, False, 0, deep), (wv_in, wv, False, 0, deep), (wq_in, wq, False, 0, deep),
+        (wo_in, wo, True, 0, half), (wo_in, wo, False, half, half),
+    )
+    n_part = len(weights)
 
     def part(a, shard):
-        rows = weights[a][0].shape[0]
-        return weights[a][1].at[pl.ds(pl.multiple_of(shard * rows, rows), rows), :]
+        source, whole, _, first, rows = weights[a]
+        start = shard * source.shape[0] + first
+        return whole.at[pl.ds(pl.multiple_of(start, rows), rows), :]
+
+    def shard_of(a):
+        return weights[a][0].at[pl.ds(weights[a][3], weights[a][4]), :]
 
     def hop(a, shard, way, own):
         there, device = around[way]
         return there, pltpu.make_async_remote_copy(
-            src_ref=weights[a][0] if own else part(a, shard),
+            src_ref=shard_of(a) if own else part(a, shard),
             dst_ref=part(a, shard),
             send_sem=g_send.at[a, shard, way],
             recv_sem=g_recv.at[a, shard],
@@ -104,7 +113,7 @@
     offsets.sort(key=lambda o: (abs(o[0]) + abs(o[1]), o))
 
     def gather(first):
-        for a in range(4):
+        for a in range(n_part):
             for way in range(4):
                 there, copy = hop(a, place, way, True)
 
@@ -117,7 +126,7 @@
 
             @pl.when(inside)
             def _(dz=dz, dx=dx, shard=zs * wide + xs):
-                for a in range(4):
+                for a in range(n_part):
                     if first:
                         hop(a, shard, 0, False)[1].wait_recv()
                     for way in ways_on(weights[a][2], dz, dx):
@@ -128,7 +137,7 @@
                             copy.start() if first else copy.wait_send()
 
     own_copies = [
-        pltpu.make_async_copy(weights[a][0], part(a, place), own_sem.at[a]) for a in range(4)
+        pltpu.make_async_copy(shard_of(a), part(a, place), own_sem.at[a]) for a in range(n_part)
     ]
     x_copy = pltpu.make_async_copy(x0_ref, xbuf, in_sem.at[0])
     g_copy = pltpu.make_async_copy(cot_ref, gbuf, in_sem.at[1])
@@ -157,6 +166,15 @@
         )
 
     n_relay = D // STEP
+    chunk = 64
+    n_back = rows_all // chunk
+
+    def relay_back(device, i):
+        rows = pl.ds(pl.multiple_of(i * chunk, chunk), chunk)
+        return pltpu.make_async_remote_copy(
+            src_ref=grad_ref.at[rows, :], dst_ref=gbuf.at[rows, :],
+            send_sem=b_send.at[i], recv_sem=b_recv.at[i], device_id=device, device_id_type=MESH,
+        )
 
     @pl.when(section == 0)
     def _():
@@ -164,10 +182,9 @@
 
     @pl.when(has_prev)
     def _():
+        gather(False)
         for c in range(n_relay):
             relay(out_ref, xbuf, x_send, x_recv, previous, c).wait_recv()
-
-    chunk = 64
 
     @pl.loop(0, rows_all // chunk)
     def _(i):
@@ -232,7 +249,7 @@
     def _():
         to_left().wait_recv()
 
-    @pl.loop(0, HEADS)
+    @pl.loop(0, HEADS, unroll=4)
     def _(h):
         cols = pl.ds(pl.multiple_of(h * HDIM, HDIM), HDIM)
         for m in range(micro):
@@ -253,29 +270,38 @@
         def _(c=c):
             relay(out_ref, xbuf, x_send, x_recv, following, c).start()
 
+    @pl.when(section == 0)
+    def _():
+        gather(False)
+
+    @pl.when(has_next)
+    def _():
+        for c in range(n_relay):
+            relay(out_ref, xbuf, x_send, x_recv, following, c).wait_send()
+
     @pl.when(section == n_section - 1)
     def _():
         g_copy.wait()
 
-    @pl.when(has_next)
-    def _():
-        for c in range(n_relay):
-            relay(grad_ref, gbuf, b_send, b_recv, following, c).wait_recv()
-
-    @pl.loop(0, WIDTH // STEP)
-    def _(i):
-        cols = pl.ds(pl.multiple_of(i * STEP, STEP), STEP)
-        datt[:, cols] = dot(gbuf[...], wo[cols, :], ((1,), (1,))).astype(BF16)
-
-    @pl.loop(0, HEADS)
-    def _(h):
-        cols = pl.ds(pl.multiple_of(h * HDIM, HDIM), HDIM)
-        for m in range(micro):
-            rows = slice(m * length, (m + 1) * length)
+    for m in range(micro):
+        rows = slice(m * length, (m + 1) * length)
+
+        @pl.when(has_next)
+        def _(m=m):
+            for i in range(m * length // chunk, (m + 1) * length // chunk):
+                relay_back(following, i).wait_recv()
+
+        @pl.loop(0, WIDTH // STEP)
+        def _(i, rows=rows):
+            cols = pl.ds(pl.multiple_of(i * STEP, STEP), STEP)
+            datt[rows, cols] = dot(gbuf[rows, :], wo[cols, :], ((1,), (1,))).astype(BF16)
+
+        @pl.loop(0, HEADS, unroll=4)
+        def _(h, m=m, rows=rows):
+            cols = pl.ds(pl.multiple_of(h * HDIM, HDIM), HDIM)
             prob = probs[m, h]
             d_att = datt[rows, cols].astype(F32)
-            inv = inv_total[rows, cols]
-            d_sum = (d_att * inv)
+            d_sum = d_att * inv_total[rows, cols]
             d_total = jnp.sum(d_sum * att[rows, cols].astype(F32), axis=-1, keepdims=True)
             d_sum = d_sum.astype(BF16)
             d_prob = dot(d_sum, kv[1, m, :, cols], ((1,), (1,))) - d_total
@@ -326,7 +352,7 @@
                 rows = slice(start, start + BLK)
                 dkv[which, m, rows] = dkv[which, m, rows] + rims[side, which, m]
 
-    @pl.loop(0, HEADS)
+    @pl.loop(0, HEADS, unroll=4)
     def _(h):
         cols = pl.ds(pl.multiple_of(h * HDIM, HDIM), HDIM)
         for m in range(micro):
@@ -356,17 +382,9 @@
         d_in = scale * (d_norm - normed * head_mean(d_norm * normed))
         grad_ref[rows, :] = (gbuf[rows, :].astype(F32) + d_in.astype(BF16).astype(F32)).astype(BF16)
 
-    @pl.when(has_prev)
-    def _():
-        for c in range(n_relay):
-            relay(grad_ref, gbuf, b_send, b_recv, previous, c).start()
-
-    gather(False)
-
-    @pl.when(has_next)
-    def _():
-        for c in range(n_relay):
-            relay(out_ref, xbuf, x_send, x_recv, following, c).wait_send()
+        @pl.when(has_prev)
+        def _():
+            relay_back(previous, i).start()
 
     @pl.when(has_right)
     def _():
@@ -380,8 +398,8 @@
 
     @pl.when(has_prev)
     def _():
-        for c in range(n_relay):
-            relay(grad_ref, gbuf, b_send, b_recv, previous, c).wait_send()
+        for i in range(n_back):
+            relay_back(previous, i).wait_send()
 
 
 def mask_weights(block_mask, place, n_ctx, length):
@@ -429,13 +447,13 @@
             pltpu.VMEM((2, micro, EXT, WIDTH), BF16),
             pltpu.VMEM((2, 2, micro, BLK, WIDTH), BF16),
             pltpu.VMEM((rows, D), F32),
-            dma((4, n_ctx)),
-            dma((4, n_ctx, 4)),
-            dma((4,)),
+            dma((5, n_ctx)),
+            dma((5, n_ctx, 4)),
+            dma((5,)),
             dma((n_relay,)),
             dma((n_relay,)),
-            dma((n_relay,)),
-            dma((n_relay,)),
+            dma((rows // 64,)),
+            dma((rows // 64,)),
             dma((2,)),
             dma((2,)),
             dma((2,)),

time: 366 us -> 347 us (0.948)
  Pallas kernels: 360 us -> 341 us
    pallas_call x1, Pallas kernels: 360 us -> 341 us  [per_device(): pl.pallas_call(functools.partial(kernel, n_section, n_ctx, micro, length)...]
where the time goes in v2:
time: 347 us
  Pallas kernels  341 us (98%)
  local copies, waits for them, and re-layouts  4.35 us (1%)
    pallas_call x1, Pallas kernels, per_device(): pl.pallas_call(functools.partial(kernel, n_section, n_ctx, micro, length)...  341 us

profile of v2, /device:TPU:16, one launch (start us, length us, event | category | flops | bytes accessed | tf_op | source)
XLA Modules:
  0.0 347.1 jit_solution(13797511111016491847)
XLA Ops:
  0.7 0.0 copy-start.1
  0.7 0.7 copy-done.1
  1.4 0.1 broadcast_in_dim.57
  1.4 0.1 broadcast_in_dim.58
  1.5 0.1 broadcast_in_dim.51
  1.6 0.1 broadcast_in_dim.52
  1.7 0.1 subtract_compare_fusion.2
  1.8 0.8 select_select_fusion.mask_ref
  2.7 341.0 %shard_map.86 = (bf16[256,2048]{1,0:T(8,128)(2,1)}, bf16[256,2048]{1,0:T(8,128)(2,1)}) custom-call(bf16[256,2048]{1,0:T(8,128)(2,1)} %bitcast.10, bf16[256,2048]{1,0:T(8,128)(2,1)} %bitcast.11, bf16[256,1024]{1,0:T(8,128)(2,1)} %bitcast.14, bf16[256,1024]{1,0:T(8,128)(2,1)} %bitcast.15, bf16[256,1024]{1,0:T(8,128)(2,1)} %bitcast.16, ...), custom_call_target="tpu_custom_call" | custom-call | tf_op jit(solution)/shard_map/pallas_call | solution.py:425
  343.7 0.0 copy-start
  343.7 2.4 copy.11
  346.1 0.0 copy-done
  346.1 1.0 copy.12
  (7 shorter events, 0.0 us)
Async XLA Ops:
  0.7 0.7 copy-start.1
  343.7 2.4 copy-start

commit v3 on v2

--- a/solution.py
+++ b/solution.py
@@ -41,7 +41,7 @@
     out_ref, grad_ref,
     wq, wk, wv, wo, xbuf, gbuf, nbuf, qbuf, rq, rk, kv, att, inv_total, probs,
     datt, dq, dkv, rims, dn,
-    g_recv, g_send, own_sem, x_recv, x_send, b_recv, b_send, h_recv, h_send, r_recv, r_send, in_sem,
+    g_recv, g_send, own_sem, x_recv, x_send, b_recv, b_send, h_recv, h_send, r_recv, r_send, in_sem, go_sem,
 ):
     section = lax.axis_index("section")
     place = lax.axis_index("ctx")
@@ -112,6 +112,9 @@
     ]
     offsets.sort(key=lambda o: (abs(o[0]) + abs(o[1]), o))
 
+    n_near = sum(abs(dz) + abs(dx) <= tall + wide - 4 for dz, dx in offsets)
+    is_first = section % 2 == 0
+
     def gather(first):
         for a in range(n_part):
             for way in range(4):
@@ -120,7 +123,11 @@
                 @pl.when(there)
                 def _(copy=copy):
                     copy.start() if first else copy.wait_send()
-        for dz, dx in offsets:
+        for spot, (dz, dx) in enumerate(offsets):
+            if first and spot == n_near:
+                @pl.when(is_first & has_next)
+                def _():
+                    pl.semaphore_signal(go_sem, inc=1, device_id=following, device_id_type=MESH)
             zs, xs = z - dz, x - dx
             inside = (zs >= 0) & (zs < tall) & (xs >= 0) & (xs < wide)
 
@@ -154,6 +161,11 @@
 
     kv[...] = jnp.zeros_like(kv)
     rims[...] = jnp.zeros_like(rims)
+
+    @pl.when(jnp.logical_not(is_first))
+    def _():
+        pl.semaphore_wait(go_sem, 1)
+
     gather(True)
     for copy in own_copies:
         copy.wait()
@@ -459,6 +471,7 @@
             dma((2,)),
             dma((2,)),
             dma((2,)),
+            pltpu.SemaphoreType.REGULAR,
         ],
         compiler_params=pltpu.CompilerParams(
             collective_id=0, has_side_effects=True, vmem_limit_bytes=56 * 2**20

time: 347 us -> 334 us (0.963)
  Pallas kernels: 341 us -> 326 us
    pallas_call x1, Pallas kernels: 341 us -> 326 us  [per_device(): pl.pallas_call(functools.partial(kernel, n_section, n_ctx, micro, length)...]
where the time goes in v3:
time: 334 us; the launch traced here: 332 us
  Pallas kernels  326 us (98%)
  local copies, waits for them, and re-layouts  4.35 us (1%)
    pallas_call x1, Pallas kernels, per_device(): pl.pallas_call(functools.partial(kernel, n_section, n_ctx, micro, length)...  326 us

profile of v3, /device:TPU:16, one launch (start us, length us, event | category | flops | bytes accessed | tf_op | source)
XLA Modules:
  0.0 332.1 jit_solution(1061687849652601842)
XLA Ops:
  0.7 0.0 copy-start.1
  0.7 0.7 copy-done.1
  1.4 0.1 broadcast_in_dim.57
  1.4 0.1 broadcast_in_dim.58
  1.5 0.1 broadcast_in_dim.51
  1.6 0.1 broadcast_in_dim.52
  1.7 0.1 subtract_compare_fusion.2
  1.8 0.8 select_select_fusion.mask_ref
  2.7 326.0 %shard_map.86 = (bf16[256,2048]{1,0:T(8,128)(2,1)}, bf16[256,2048]{1,0:T(8,128)(2,1)}) custom-call(bf16[256,2048]{1,0:T(8,128)(2,1)} %bitcast.10, bf16[256,2048]{1,0:T(8,128)(2,1)} %bitcast.11, bf16[256,1024]{1,0:T(8,128)(2,1)} %bitcast.14, bf16[256,1024]{1,0:T(8,128)(2,1)} %bitcast.15, bf16[256,1024]{1,0:T(8,128)(2,1)} %bitcast.16, ...), custom_call_target="tpu_custom_call" | custom-call | tf_op jit(solution)/shard_map/pallas_call | solution.py:437
  328.7 0.0 copy-start
  328.7 2.4 copy.11
  331.1 0.0 copy-done
  331.1 1.0 copy.12
  (7 shorter events, 0.0 us)
Async XLA Ops:
  0.7 0.7 copy-start.1
  328.7 2.4 copy-start

commit v4 on v3

--- a/solution.py
+++ b/solution.py
@@ -39,7 +39,7 @@
     n_section, n_ctx, micro, length,
     x0_ref, cot_ref, wq_in, wk_in, wv_in, wo_in, mask_ref,
     out_ref, grad_ref,
-    wq, wk, wv, wo, xbuf, gbuf, nbuf, qbuf, rq, rk, kv, att, inv_total, probs,
+    wq, wk, wv, wo, wq_t, wk_t, wv_t, wo_t, xbuf, gbuf, nbuf, qbuf, rq, rk, kv, att, inv_total, probs,
     datt, dq, dkv, rims, dn,
     g_recv, g_send, own_sem, x_recv, x_send, b_recv, b_send, h_recv, h_send, r_recv, r_send, in_sem, go_sem,
 ):
@@ -191,6 +191,22 @@
     @pl.when(section == 0)
     def _():
         x_copy.wait()
+
+    def turn():
+        @pl.loop(0, D // EXT)
+        def _(i):
+            rows = pl.ds(pl.multiple_of(i * EXT, EXT), EXT)
+            for whole, turned in ((wq, wq_t), (wk, wk_t), (wv, wv_t)):
+                turned[:, rows] = whole[rows, :].T
+
+        @pl.loop(0, WIDTH // EXT)
+        def _(i):
+            rows = pl.ds(pl.multiple_of(i * EXT, EXT), EXT)
+            wo_t[:, rows] = wo[rows, :].T
+
+    @pl.when(section >= 2)
+    def _():
+        turn()
 
     @pl.when(has_prev)
     def _():
@@ -282,6 +298,10 @@
         def _(c=c):
             relay(out_ref, xbuf, x_send, x_recv, following, c).start()
 
+    @pl.when(section < 2)
+    def _():
+        turn()
+
     @pl.when(section == 0)
     def _():
         gather(False)
@@ -306,7 +326,7 @@
         @pl.loop(0, WIDTH // STEP)
         def _(i, rows=rows):
             cols = pl.ds(pl.multiple_of(i * STEP, STEP), STEP)
-            datt[rows, cols] = dot(gbuf[rows, :], wo[cols, :], ((1,), (1,))).astype(BF16)
+            datt[rows, cols] = dot(gbuf[rows, :], wo_t[:, cols]).astype(BF16)
 
         @pl.loop(0, HEADS, unroll=4)
         def _(h, m=m, rows=rows):
@@ -348,7 +368,7 @@
     @pl.loop(0, D // STEP)
     def _(i):
         cols = pl.ds(pl.multiple_of(i * STEP, STEP), STEP)
-        dn[:, cols] = dot(dq[...], wq[cols, :], ((1,), (1,)))
+        dn[:, cols] = dot(dq[...], wq_t[:, cols])
 
     @pl.when(has_right)
     def _():
@@ -380,8 +400,8 @@
         cols = pl.ds(pl.multiple_of(i * STEP, STEP), STEP)
         dn[:, cols] = (
             dn[:, cols]
-            + dot(dq[...], wk[cols, :], ((1,), (1,)))
-            + dot(datt[...], wv[cols, :], ((1,), (1,)))
+            + dot(dq[...], wk_t[:, cols])
+            + dot(datt[...], wv_t[:, cols])
         )
 
     @pl.loop(0, rows_all // chunk)
@@ -444,6 +464,10 @@
             pltpu.VMEM((D, WIDTH), BF16),
             pltpu.VMEM((D, WIDTH), BF16),
             pltpu.VMEM((WIDTH, D), BF16),
+            pltpu.VMEM((WIDTH, D), BF16),
+            pltpu.VMEM((WIDTH, D), BF16),
+            pltpu.VMEM((WIDTH, D), BF16),
+            pltpu.VMEM((D, WIDTH), BF16),
             pltpu.VMEM((rows, D), BF16),
             pltpu.VMEM((rows, D), BF16),
             pltpu.VMEM((rows, D), BF16),
@@ -474,7 +498,7 @@
             pltpu.SemaphoreType.REGULAR,
         ],
         compiler_params=pltpu.CompilerParams(
-            collective_id=0, has_side_effects=True, vmem_limit_bytes=56 * 2**20
+            collective_id=0, has_side_effects=True, vmem_limit_bytes=60 * 2**20
         ),
     )(
         section_input.reshape(rows, D), cotangent.reshape(rows, D),

time: 334 us -> 329 us (0.985)
  Pallas kernels: 326 us -> 320 us
    pallas_call x1, Pallas kernels: 326 us -> 320 us  [per_device(): pl.pallas_call(functools.partial(kernel, n_section, n_ctx, micro, length)...]
where the time goes in v4:
time: 329 us; the launch traced here: 326 us
  Pallas kernels  320 us (97%)
  local copies, waits for them, and re-layouts  4.35 us (1%)
    pallas_call x1, Pallas kernels, per_device(): pl.pallas_call(functools.partial(kernel, n_section, n_ctx, micro, length)...  320 us

profile of v4, /device:TPU:16, one launch (start us, length us, event | category | flops | bytes accessed | tf_op | source)
XLA Modules:
  0.0 326.3 jit_solution(17857448810816244224)
XLA Ops:
  0.7 0.0 copy-start.1
  0.7 0.7 copy-done.1
  1.4 0.1 broadcast_in_dim.57
  1.4 0.1 broadcast_in_dim.58
  1.5 0.1 broadcast_in_dim.51
  1.6 0.1 broadcast_in_dim.52
  1.7 0.1 subtract_compare_fusion.2
  1.8 0.8 select_select_fusion.mask_ref
  2.7 320.3 %shard_map.86 = (bf16[256,2048]{1,0:T(8,128)(2,1)}, bf16[256,2048]{1,0:T(8,128)(2,1)}) custom-call(bf16[256,2048]{1,0:T(8,128)(2,1)} %bitcast.10, bf16[256,2048]{1,0:T(8,128)(2,1)} %bitcast.11, bf16[256,1024]{1,0:T(8,128)(2,1)} %bitcast.14, bf16[256,1024]{1,0:T(8,128)(2,1)} %bitcast.15, bf16[256,1024]{1,0:T(8,128)(2,1)} %bitcast.16, ...), custom_call_target="tpu_custom_call" | custom-call | tf_op jit(solution)/shard_map/pallas_call | solution.py:457
  322.9 0.0 copy-start
  323.0 2.4 copy.11
  325.3 0.0 copy-done
  325.4 1.0 copy.12
  (7 shorter events, 0.0 us)
Async XLA Ops:
  0.7 0.7 copy-start.1
  322.9 2.4 copy-start
